TPU v7x, 32 devices: a whole 2x2x4 slice. The times are simulated.
32 devices in a mesh: ctx: 8 (over z, x), head: 4 (over y, core).
Axes of the slice: x: 2, y: 2, z: 4, core: 2. Of those that a mesh axis runs over, the one named last changes fastest.
Arguments:
- x_raw: bfloat16 [2048, 4096], P('ctx', 'head'), may hold values from -30 to 30
- bc_raw: bfloat16 [2048, 256], P('ctx'), may hold values from -6 to 6
- gate_raw: bfloat16 [2048, 4096], P('ctx', 'head'), may hold values from -16 to 16
- log_decay: float32 [64, 2048], P('head', 'ctx'), may hold values from -0.8 to 0
- level_weights: float32 [16, 64, 2048], P(None, 'head', 'ctx'), may hold values from 0.25 to 2
- conv_x: float32 [4, 4096], P(None, 'head'), may hold values from -3 to 3
- conv_bc: float32 [4, 256], replicated, may hold values from -3 to 3
- norm_gain: float32 [4096], P('head'), may hold values from 0.5 to 1.5
- out_grad: bfloat16 [2048, 4096], P('ctx', 'head'), may hold values from -6 to 6
Outputs:
- layer_out: bfloat16 [2048, 4096], P('ctx', 'head')
- x_grad: bfloat16 [2048, 4096], P('ctx', 'head')
- bc_grad: bfloat16 [2048, 256], P('ctx')
All inputs are finite; a program needn't handle non-finite values.
Results may differ from a plain program's by a relative error of at most 0.0013.
Values may be sent and summed in bfloat16 or wider, within the bound.
No kernel may reach another device: no remote copies, remote signals or barrier semaphores. Data moves between devices by JAX's collectives and lax.ppermute only.
A program may use at most 128 MiB of HBM per device.

v0:
```python
import jax
import jax.numpy as jnp
from jax import lax
from jax.sharding import PartitionSpec as P

HEADS = 64
HEAD_DIM = 64
STATE = 128


highest = lax.Precision.HIGHEST
epsilon = 1e-05


def shifted(value, axis, steps):
    count = lax.axis_size(axis)
    initial, last = (max(0, -steps), min(count, count - steps))
    return lax.ppermute(value, axis, [(source, source + steps) for source in range(initial, last)])


def from_partner(block, axis, distance):
    count = lax.axis_size(axis)
    route = []
    for low in range(count):
        high = low | 1 << distance
        if high != low and high < count:
            route += [(low, high), (high, low)]
    return lax.ppermute(block, axis, route)


def matmul(left_mat, right_mat):
    return jnp.dot(left_mat, right_mat, precision=highest, preferred_element_type=jnp.float32)


def silu_slope(pre_act):
    sigmoid_val = jax.nn.sigmoid(pre_act)
    return sigmoid_val * (1.0 + pre_act * (1.0 - sigmoid_val))


def bit_length(values, count):
    summed = jnp.zeros(values.shape, jnp.int32)
    for bit_pos in range(count):
        summed = summed + (values >= 2**bit_pos).astype(jnp.int32)
    return summed


def per_column(values, head_dim):
    return jnp.repeat(values, head_dim, axis=0)


def conv_forward(raw_rows, rim_rows, weights):
    padded = jnp.concatenate([rim_rows, raw_rows], axis=0).astype(jnp.float32)
    length = raw_rows.shape[0]
    summed = jnp.zeros(raw_rows.shape, jnp.float32)
    for tap_id in range(weights.shape[0]):
        summed = summed + weights[tap_id] * padded[tap_id : tap_id + length]
    return summed


def conv_backward(slope_rows, next_rows, weights):
    extended = jnp.concatenate([slope_rows, next_rows], axis=0)
    length = slope_rows.shape[0]
    tap_count = weights.shape[0]
    summed = jnp.zeros(slope_rows.shape, jnp.float32)
    for tap_id in range(tap_count):
        offset = tap_count - 1 - tap_id
        summed = summed + weights[tap_id] * extended[offset : offset + length]
    return summed


def head_mix(cum_head, weight_head, inside, causal, low_bits):
    chosen = jnp.zeros(inside.shape, jnp.float32)
    for levels_id in range(low_bits + 1):
        chosen = jnp.where(inside == levels_id, weight_head[levels_id][:, None], chosen)
    exponent = jnp.where(causal, cum_head[:, None] - cum_head[None, :], -jnp.inf)
    return chosen * jnp.exp(exponent)


def per_device(
    x_raw, bc_raw, gate_raw, log_decay, level_weights, conv_x, conv_bc, norm_gain, out_grad
):
    length = x_raw.shape[0]
    columns = x_raw.shape[1]
    head_count = log_decay.shape[0]
    head_dim = HEAD_DIM
    state_dim = STATE
    tap_count = conv_x.shape[0]
    low_bits = length.bit_length() - 1
    level_count = level_weights.shape[0]
    ctx_bits = lax.axis_size("ctx").bit_length() - 1
    ctx_rank = lax.axis_index("ctx")
    inner_width = HEADS * HEAD_DIM
    x_rim, bc_rim = shifted(
        (x_raw[length - tap_count + 1 :], bc_raw[length - tap_count + 1 :]), "ctx", 1
    )
    x_pre = conv_forward(x_raw, x_rim, conv_x)
    bc_pre = conv_forward(bc_raw, bc_rim, conv_bc)
    x_conv = jax.nn.silu(x_pre)
    bc_conv = jax.nn.silu(bc_pre)
    b_conv = bc_conv[:, :state_dim]
    c_conv = bc_conv[:, state_dim:]
    cum_decay = jnp.cumsum(log_decay, axis=1)
    summed = cum_decay[:, -1]
    end_weight = per_column(jnp.exp(summed[:, None] - cum_decay), head_dim).T
    x_weighted = x_conv * end_weight
    end_state = matmul(b_conv.T, x_weighted)
    position = jnp.arange(length, dtype=jnp.int32)
    inside = bit_length(jnp.bitwise_xor(position[:, None], position[None, :]), low_bits)
    causal = position[:, None] >= position[None, :]
    scores = matmul(c_conv, b_conv.T)

    def intra_forward(head_id, accumulated):
        weights = head_mix(
            cum_decay[head_id],
            lax.dynamic_index_in_dim(level_weights, head_id, 1, keepdims=False),
            inside,
            causal,
            low_bits,
        )
        values = lax.dynamic_slice_in_dim(x_conv, head_id * head_dim, head_dim, 1)
        result = matmul(weights * scores, values)
        return lax.dynamic_update_slice_in_dim(accumulated, result, head_id * head_dim, 1)

    intra = lax.fori_loop(0, head_count, intra_forward, jnp.zeros((length, columns), jnp.float32))
    bit_flags = jnp.stack([ctx_rank // 2**bit_pos % 2 for bit_pos in range(ctx_bits)]).astype(
        jnp.float32
    )
    far_weights = jnp.stack(
        [level_weights[min(low_bits + 1 + bit_pos, level_count - 1)] for bit_pos in range(ctx_bits)]
    )
    far_coef = far_weights * jnp.exp(cum_decay)[None] * bit_flags[:, None, None]
    coef_wide = (
        jnp.repeat(far_coef, head_dim, axis=1)
        .transpose(2, 0, 1)
        .reshape(length, ctx_bits * columns)
    )

    def fenwick_states(state_in, total_in):
        block_state = state_in
        block_total = total_in
        before = jnp.zeros(total_in.shape, jnp.float32)
        collected = []
        own_list = []
        other_list = []
        for bit_pos in range(ctx_bits):
            other_state, other_total = from_partner((block_state, block_total), "ctx", bit_pos)
            upper_half = bit_flags[bit_pos]
            collected.append(upper_half * other_state * per_column(jnp.exp(before), head_dim))
            own_list.append(block_total)
            other_list.append(other_total)
            joined_upper = other_state * per_column(jnp.exp(block_total), head_dim) + block_state
            joined_lower = block_state * per_column(jnp.exp(other_total), head_dim) + other_state
            block_state = upper_half * joined_upper + (1.0 - upper_half) * joined_lower
            before = before + upper_half * other_total
            block_total = block_total + other_total
        return (jnp.concatenate(collected, axis=1), own_list, other_list)

    far_states, own_totals, other_totals = fenwick_states(end_state, summed)
    projected = matmul(c_conv, far_states)
    inter = jnp.sum((projected * coef_wide).reshape(length, ctx_bits, columns), axis=1)
    ssd_out = intra + inter
    gate_act = jax.nn.silu(gate_raw.astype(jnp.float32))
    mixed = ssd_out * gate_act
    scaled_grad = norm_gain * out_grad.astype(jnp.float32)
    square_sum, cross_sum = lax.psum(
        (jnp.sum(mixed * mixed, axis=1), jnp.sum(scaled_grad * mixed, axis=1)), "head"
    )
    inverse = lax.rsqrt(square_sum / inner_width + epsilon)[:, None]
    layer_out = (norm_gain * mixed * inverse).astype(jnp.bfloat16)
    mixed_grad = scaled_grad * inverse - mixed * inverse**3 * (cross_sum[:, None] / inner_width)
    ssd_grad = mixed_grad * gate_act

    def intra_backward(head_id, running):
        conv_acc, score_grad = running
        weights = head_mix(
            cum_decay[head_id],
            lax.dynamic_index_in_dim(level_weights, head_id, 1, keepdims=False),
            inside,
            causal,
            low_bits,
        )
        values = lax.dynamic_slice_in_dim(x_conv, head_id * head_dim, head_dim, 1)
        grad_rows = lax.dynamic_slice_in_dim(ssd_grad, head_id * head_dim, head_dim, 1)
        mixing = weights * scores
        conv_acc = lax.dynamic_update_slice_in_dim(
            conv_acc, matmul(mixing.T, grad_rows), head_id * head_dim, 1
        )
        score_grad = score_grad + matmul(grad_rows, values.T) * weights
        return (conv_acc, score_grad)

    conv_grad, score_grad = lax.fori_loop(
        0,
        head_count,
        intra_backward,
        (jnp.zeros((length, columns), jnp.float32), jnp.zeros((length, length), jnp.float32)),
    )
    c_grad = matmul(score_grad, b_conv)
    input_matrix_derivative = matmul(score_grad.T, c_conv)
    again_state = matmul(b_conv.T, x_conv * end_weight)
    used_states, used_own, used_other = fenwick_states(again_state, summed)
    far_grad = jnp.tile(ssd_grad, (1, ctx_bits)) * coef_wide
    c_grad = c_grad + matmul(far_grad, used_states.T)
    level_grads = matmul(c_conv.T, far_grad)
    stack_now = level_grads
    received = jnp.zeros((state_dim, columns), jnp.float32)
    after = jnp.zeros((head_count,), jnp.float32)
    for bit_pos in range(ctx_bits):
        other_stack = from_partner(stack_now, "ctx", bit_pos)
        upper_half = bit_flags[bit_pos]
        remaining = ctx_bits - bit_pos
        received = received + (1.0 - upper_half) * other_stack[:, :columns] * per_column(
            jnp.exp(after), head_dim
        )
        own_scale = jnp.tile(per_column(jnp.exp(used_own[bit_pos]), head_dim), remaining)
        other_scale = jnp.tile(per_column(jnp.exp(used_other[bit_pos]), head_dim), remaining)
        merged = upper_half * (other_stack + other_scale * stack_now) + (1.0 - upper_half) * (
            stack_now + own_scale * other_stack
        )
        stack_now = merged[:, columns:]
        after = after + (1.0 - upper_half) * used_other[bit_pos]
    conv_grad = conv_grad + matmul(b_conv, received) * end_weight
    input_matrix_derivative = input_matrix_derivative + matmul(x_weighted, received.T)
    x_slope = conv_grad * silu_slope(x_pre)
    bc_slope_act = silu_slope(bc_pre)
    bc_slope = jnp.concatenate([input_matrix_derivative, c_grad], axis=1) * bc_slope_act
    x_next, bc_next = shifted((x_slope[: tap_count - 1], bc_slope[: tap_count - 1]), "ctx", -1)
    x_grad = conv_backward(x_slope, x_next, conv_x)
    bc_grad = lax.psum(conv_backward(bc_slope, bc_next, conv_bc), "head")
    return (layer_out, x_grad.astype(jnp.bfloat16), bc_grad.astype(jnp.bfloat16))


def solution(mesh):
    in_specs = (
        P("ctx", "head"),
        P("ctx", None),
        P("ctx", "head"),
        P("head", "ctx"),
        P(None, "head", "ctx"),
        P(None, "head"),
        P(),
        P("head"),
        P("ctx", "head"),
    )
    out_specs = (P("ctx", "head"), P("ctx", "head"), P("ctx", None))
    return jax.shard_map(
        per_device, mesh=mesh, in_specs=in_specs, out_specs=out_specs, check_vma=False
    )
```

profile of v0, /device:TPU:0, one launch (start us, length us, event | category | flops | bytes accessed | tf_op | source)
XLA Modules:
  0.0 318.6 jit_solution(13758080019870608056)
XLA Ops:
  1.5 4.8 %collective-permute-start = (bf16[3,256]{0,1:T(8,128)(2,1)S(1)}, bf16[3,256]{0,1:T(8,128)(2,1)S(1)}, u32[]{:S(2)}, u32[]{:S(2)}) collective-permute-start(bf16[3,256]{0,1:T(8,128)(2,1)S(1)} %copy.33), channel_id=1, source_target_pairs={{0,4},{4,8},{8,12},{12,16},{16,20},{20,24},{24,28},{1,5},{5,9},{9,... | collective-permute-start | bytes 4616 | tf_op jit(solution)/shard_map/ppermute | solution.py:18
  7.1 3.4 %collective-permute-start.1 = (bf16[3,1024]{1,0:T(4,128)(2,1)S(1)}, bf16[3,1024]{1,0:T(4,128)(2,1)S(1)}, u32[]{:S(2)}, u32[]{:S(2)}) collective-permute-start(bf16[3,1024]{1,0:T(4,128)(2,1)S(1)} %slice.292), channel_id=1, source_target_pairs={{0,4},{4,8},{8,12},{12,16},{16,20},{20,24},{24,28},{1,5},{5,9},{9,... | collective-permute-start | bytes 18440 | tf_op jit(solution)/shard_map/ppermute | solution.py:18
  25.1 1.8 collective-permute-done.5
  26.9 1.9 add_exponential_fusion
  28.9 4.6 %collective-permute-done.2 = f32[128,1024]{1,0:T(8,128)S(1)} collective-permute-done((f32[128,1024]{1,0:T(8,128)S(1)}, f32[128,1024]{1,0:T(8,128)S(1)}, u32[]{:S(2)}, u32[]{:S(2)}) %collective-permute-start.2) | collective-permute-done | bytes 524320 | tf_op jit(solution)/shard_map/ppermute | solution.py:28
  33.6 1.7 broadcast_multiply_fusion
  38.0 2.3 copy.36
  41.3 6.2 %collective-permute-done.4 = f32[128,1024]{1,0:T(8,128)} collective-permute-done((f32[128,1024]{1,0:T(8,128)}, f32[128,1024]{1,0:T(8,128)}, u32[]{:S(2)}, u32[]{:S(2)}) %collective-permute-start.4) | collective-permute-done | bytes 524320 | tf_op jit(solution)/shard_map/ppermute | solution.py:28
  47.5 3.0 multiply_multiply_fusion.1
  50.6 2.6 collective-permute-start.6
  53.2 41.5 %while.32 = (s32[]{:T(128)}, f32[256,1024]{0,1:T(8,128)S(1)}, f32[16,16,256]{2,1,0:T(8,128)}, f32[16,256]{1,0:T(8,128)S(1)}, f32[256,256]{1,0:T(8,128)S(1)}, /*i...) while((s32[]{:T(128)}, f32[256,1024]{0,1:T(8,128)S(1)}, ...), condition=%wide.region_3.4_spmd.clone.clone, body=%wide.region_2.3_spmd.clone.clone.sunk | while | flops 53411852 | bytes 491875 | solution.py:124
  56.7 1.7 convolution_dynamic-update-slice_fusion.4
  64.5 1.7 convolution_dynamic-update-slice_fusion.4
  69.7 1.7 convolution_dynamic-update-slice_fusion.4
  80.0 1.7 convolution_dynamic-update-slice_fusion.4
  85.2 1.7 convolution_dynamic-update-slice_fusion.4
  96.4 2.7 copy.38
  101.6 5.5 %convolution_multiply_fusion.1 = f32[256,3072]{1,0:T(8,128)} fusion(f32[256,3072]{1,0:T(8,128)S(1)} %copy-done.1, f32[128,1024]{1,0:T(8,128)S(1)} %multiply_multiply_fusion, f32[128,1024]{1,0:T(8,128)} %get-tuple-element.537, f32[128,1024]{1,0:T(8,128)} %get-tuple-element.535, f32[256,256]{0,1:T(8,128)S(1)} %get-tuple-element.513), kind=kOutput, calls=%fused_computation.136 | convolution fusion | flops 1209532416 | bytes 7995392 | tf_op jit(solution)/shard_map/dot_general | solution.py:32
  107.1 2.4 copy.37
  112.5 1.8 multiply_reduce_fusion
  114.3 5.8 %all-reduce = (f32[256]{0:T(256)S(1)}, f32[256]{0:T(256)S(1)}) all-reduce(f32[256]{0:T(256)S(1)} %get-tuple-element.477, f32[256]{0:T(256)S(1)} %get-tuple-element.476), channel_id=1, replica_groups=mesh['ctx'=8,'head'=4] {'head'}, use_global_device_ids=true, to_apply=%region_6.7 | all-reduce | flops 512 | bytes 4096 | tf_op jit(solution)/shard_map/psum | solution.py:165
  120.1 2.6 subtract_multiply_fusion
  126.5 4.5 %fusion.152 = f32[128,3072]{1,0:T(8,128)} fusion(f32[256,3072]{0,1:T(8,128)S(1)} %bitcast_multiply_fusion, f32[256,256]{0,1:T(8,128)S(1)} %get-tuple-element.513), kind=kOutput, calls=%fused_computation.223 | convolution fusion | flops 1207959552 | bytes 4849664 | tf_op jit(solution)/shard_map/dot_general | solution.py:32
  132.6 34.9 %collective-permute-done.7 = f32[128,3072]{1,0:T(8,128)} collective-permute-done((f32[128,3072]{1,0:T(8,128)}, f32[128,3072]{1,0:T(8,128)}, u32[]{:S(2)}, u32[]{:S(2)}) %collective-permute-start.7) | collective-permute-done | bytes 1572896 | tf_op jit(solution)/shard_map/ppermute | solution.py:28
  167.5 3.5 %multiply_add_fusion = f32[128,2048]{1,0:T(8,128)} fusion(f32[128,3072]{1,0:T(8,128)} %collective-permute-done.7, f32[128,3072]{1,0:T(8,128)} %fusion.152, f32[]{:T(128)S(6)} %sub.127, f32[]{:T(128)} %bitcast.11, f32[2048]{0:T(1024)S(1)} %slice.368, f32[2048]{0:T(1024)S(1)} %slice.366), kind=kLoop, calls=%fused_computation.169 | loop fusion | flops 1835008 | bytes 3162120 | tf_op jit(solution)/shard_map/add | solution.py:216
  172.3 89.7 %while.33 = (s32[]{:T(128)}, f32[256,1024]{0,1:T(8,128)}, f32[256,256]{1,0:T(8,128)}, f32[16,16,256]{2,1,0:T(8,128)}, f32[16,256]{1,0:T(8,128)S(1)}, /*index=5*/...) while((s32[]{:T(128)}, f32[256,1024]{0,1:T(8,128)}, ...), condition=%wide.region_10.11_spmd.clone.clone, body=%wide.region_9.10_spmd.clone.clone.sunk | while | flops 106954768 | bytes 1291132 | solution.py:191
  173.2 2.4 convolution_dynamic-update-slice_fusion.5
  175.6 2.2 fusion.187
  178.7 2.4 convolution_dynamic-update-slice_fusion.5
  181.1 2.3 fusion.187
  184.3 2.4 convolution_dynamic-update-slice_fusion.5
  186.7 2.3 fusion.187
  189.9 2.4 convolution_dynamic-update-slice_fusion.5
  192.4 2.3 fusion.187
  195.6 2.4 convolution_dynamic-update-slice_fusion.5
  198.0 2.3 fusion.187
  201.2 2.4 convolution_dynamic-update-slice_fusion.5
  203.6 2.3 fusion.187
  206.8 2.4 convolution_dynamic-update-slice_fusion.5
  209.2 2.3 fusion.187
  212.4 2.4 convolution_dynamic-update-slice_fusion.5
  214.8 2.3 fusion.187
  218.0 2.4 convolution_dynamic-update-slice_fusion.5
  220.5 2.3 fusion.187
  223.6 2.4 convolution_dynamic-update-slice_fusion.5
  226.1 2.3 fusion.187
  229.2 2.4 convolution_dynamic-update-slice_fusion.5
  231.7 2.3 fusion.187
  234.9 2.4 convolution_dynamic-update-slice_fusion.5
  237.3 2.3 fusion.187
  240.5 2.4 convolution_dynamic-update-slice_fusion.5
  242.9 2.3 fusion.187
  246.1 2.4 convolution_dynamic-update-slice_fusion.5
  248.5 2.3 fusion.187
  251.7 2.4 convolution_dynamic-update-slice_fusion.5
  254.1 2.3 fusion.187
  257.3 2.4 convolution_dynamic-update-slice_fusion.5
  259.7 2.3 fusion.187
  262.1 2.5 copy.41
  266.1 2.0 multiply_add_fusion.1
  270.2 1.9 convolution_add_fusion
  272.1 20.7 %collective-permute-done.9 = f32[128,1024]{1,0:T(8,128)S(1)} collective-permute-done((f32[128,1024]{1,0:T(8,128)S(1)}, f32[128,1024]{1,0:T(8,128)S(1)}, u32[]{:S(2)}, u32[]{:S(2)}) %collective-permute-start.9) | collective-permute-done | bytes 524320 | tf_op jit(solution)/shard_map/ppermute | solution.py:28
  299.7 3.1 collective-permute-done.11
  303.3 13.3 %all-reduce.2 = bf16[256,256]{0,1:T(8,128)(2,1)S(1)} all-reduce(f32[256,256]{0,1:T(8,128)S(1)} %fusion.136), channel_id=1, replica_groups=mesh['ctx'=8,'head'=4] {'head'}, use_global_device_ids=true, to_apply=%region_11.12 | all-reduce | flops 65536 | bytes 393216 | tf_op jit(solution)/shard_map/psum | solution.py:228
  (207 shorter events, 90.7 us)
Async XLA Ops:
  0.6 9.9 %copy-start = (f32[16,256]{1,0:T(8,128)S(1)}, f32[16,256]{1,0:T(8,128)}, u32[]{:S(2)}) copy-start(f32[16,256]{1,0:T(8,128)} %param.16) | copy-start | bytes 49156
  1.5 15.0 %collective-permute-start = (bf16[3,256]{0,1:T(8,128)(2,1)S(1)}, bf16[3,256]{0,1:T(8,128)(2,1)S(1)}, u32[]{:S(2)}, u32[]{:S(2)}) collective-permute-start(bf16[3,256]{0,1:T(8,128)(2,1)S(1)} %copy.33), channel_id=1, source_target_pairs={{0,4},{4,8},{8,12},{12,16},{16,20},{20,24},{24,28},{1,5},{5,9},{9,... | collective-permute-start | bytes 4616 | tf_op jit(solution)/shard_map/ppermute | solution.py:18
  7.1 10.7 %collective-permute-start.1 = (bf16[3,1024]{1,0:T(4,128)(2,1)S(1)}, bf16[3,1024]{1,0:T(4,128)(2,1)S(1)}, u32[]{:S(2)}, u32[]{:S(2)}) collective-permute-start(bf16[3,1024]{1,0:T(4,128)(2,1)S(1)} %slice.292), channel_id=1, source_target_pairs={{0,4},{4,8},{8,12},{12,16},{16,20},{20,24},{24,28},{1,5},{5,9},{9,... | collective-permute-start | bytes 18440 | tf_op jit(solution)/shard_map/ppermute | solution.py:18
  11.6 11.7 %collective-permute-start.3 = (f32[16]{0:T(128)S(1)}, f32[16]{0:T(128)S(1)}, u32[]{:S(2)}, u32[]{:S(2)}) collective-permute-start(f32[16]{0:T(128)S(1)} %slice_reduce_fusion.1), channel_id=1, source_target_pairs={{0,4},{4,0},{8,12},{12,8},{16,20},{20,16},{24,28},{28,24},{1,5},{5... | collective-permute-start | bytes 200 | tf_op jit(solution)/shard_map/ppermute | solution.py:28
  16.5 3.2 %copy-start.9 = (f32[1024,256]{0,1:T(8,128)}, f32[1024,256]{0,1:T(8,128)S(1)}, u32[]{:S(2)}) copy-start(f32[1024,256]{0,1:T(8,128)S(1)} %copy.35) | copy-start | bytes 3145732
  16.5 1.4 copy-start.16
  19.7 1.0 copy-start.14
  20.7 12.9 %collective-permute-start.2 = (f32[128,1024]{1,0:T(8,128)S(1)}, f32[128,1024]{1,0:T(8,128)S(1)}, u32[]{:S(2)}, u32[]{:S(2)}) collective-permute-start(f32[128,1024]{1,0:T(8,128)S(1)} %fusion.131), channel_id=1, source_target_pairs={{0,4},{4,0},{8,12},{12,8},{16,20},{20,16},{24,28},{28,24},{1,5},{5... | collective-permute-start | bytes 1572872 | tf_op jit(solution)/shard_map/ppermute | solution.py:28
  23.3 3.6 %collective-permute-start.5 = (f32[16]{0:T(128)S(1)}, f32[16]{0:T(128)S(1)}, u32[]{:S(2)}, u32[]{:S(2)}) collective-permute-start(f32[16]{0:T(128)S(1)} %get-tuple-element.510), channel_id=1, source_target_pairs={{0,8},{8,0},{4,12},{12,4},{16,24},{24,16},{20,28},{28,20},{1,9},{9... | collective-permute-start | bytes 200 | tf_op jit(solution)/shard_map/ppermute | solution.py:28
  35.3 12.2 %collective-permute-start.4 = (f32[128,1024]{1,0:T(8,128)}, f32[128,1024]{1,0:T(8,128)}, u32[]{:S(2)}, u32[]{:S(2)}) collective-permute-start(f32[128,1024]{1,0:T(8,128)} %get-tuple-element.536), channel_id=1, source_target_pairs={{0,8},{8,0},{4,12},{12,4},{16,24},{24,16},{20,28},{28,20},{1,9},{9... | collective-permute-start | bytes 1572872 | tf_op jit(solution)/shard_map/ppermute | solution.py:28
  38.0 2.5 copy-start.20
  50.6 48.6 %collective-permute-start.6 = (f32[128,1024]{1,0:T(8,128)}, f32[128,1024]{1,0:T(8,128)}, u32[]{:S(2)}, u32[]{:S(2)}) collective-permute-start(f32[128,1024]{1,0:T(8,128)} %get-tuple-element.538), channel_id=1, source_target_pairs={{0,16},{16,0},{4,20},{20,4},{8,24},{24,8},{12,28},{28,12},{1,17},{... | collective-permute-start | bytes 1572872 | tf_op jit(solution)/shard_map/ppermute | solution.py:28
  94.7 1.1 copy-start.8
  95.7 0.7 copy-start.17
  96.4 5.2 %copy-start.1 = (f32[256,3072]{1,0:T(8,128)S(1)}, f32[256,3072]{1,0:T(8,128)}, u32[]{:S(2)}) copy-start(f32[256,3072]{1,0:T(8,128)} %copy.36) | copy-start | bytes 9437188
  100.8 0.8 copy-start.4
  110.8 1.7 copy-start.7
  110.8 1.7 copy-start.18
  122.7 1.0 copy-start.6
  126.5 5.8 %copy-start.19 = (f32[16]{0:T(128)S(1)}, f32[16]{0:T(128)}, u32[]{:S(2)}) copy-start(f32[16]{0:T(128)} %get-tuple-element.549) | copy-start | bytes 196
  131.0 36.5 %collective-permute-start.7 = (f32[128,3072]{1,0:T(8,128)}, f32[128,3072]{1,0:T(8,128)}, u32[]{:S(2)}, u32[]{:S(2)}) collective-permute-start(f32[128,3072]{1,0:T(8,128)} %fusion.152), channel_id=1, source_target_pairs={{0,4},{4,0},{8,12},{12,8},{16,20},{20,16},{24,28},{28,24},{1,5},{5... | collective-permute-start | bytes 4718600 | tf_op jit(solution)/shard_map/ppermute | solution.py:28
  171.0 95.2 %collective-permute-start.8 = (f32[128,2048]{1,0:T(8,128)}, f32[128,2048]{1,0:T(8,128)}, u32[]{:S(2)}, u32[]{:S(2)}) collective-permute-start(f32[128,2048]{1,0:T(8,128)} %multiply_add_fusion), channel_id=1, source_target_pairs={{0,8},{8,0},{4,12},{12,4},{16,24},{24,16},{20,28},{28,20},{1,9},{9... | collective-permute-start | bytes 3145736 | tf_op jit(solution)/shard_map/ppermute | solution.py:28
  264.6 5.2 %copy-start.13 = (f32[256,256]{1,0:T(8,128)S(1)}, f32[256,256]{1,0:T(8,128)}, u32[]{:S(2)}) copy-start(f32[256,256]{1,0:T(8,128)} %get-tuple-element.362) | copy-start | bytes 786436
  264.6 5.5 %copy-start.2 = (f32[128,1024]{1,0:T(8,128)S(1)}, f32[128,1024]{1,0:T(8,128)}, u32[]{:S(2)}) copy-start(f32[128,1024]{1,0:T(8,128)} %get-tuple-element.535) | copy-start | bytes 1572868
  264.6 5.5 %copy-start.3 = (f32[128,1024]{1,0:T(8,128)S(1)}, f32[128,1024]{1,0:T(8,128)}, u32[]{:S(2)}) copy-start(f32[128,1024]{1,0:T(8,128)} %get-tuple-element.537) | copy-start | bytes 1572868
  264.6 5.6 %copy-start.5 = (f32[128,1024]{1,0:T(8,128)S(1)}, f32[128,1024]{1,0:T(8,128)}, u32[]{:S(2)}) copy-start(f32[128,1024]{1,0:T(8,128)} %copy-done.4) | copy-start | bytes 1572868
  268.1 24.7 %collective-permute-start.9 = (f32[128,1024]{1,0:T(8,128)S(1)}, f32[128,1024]{1,0:T(8,128)S(1)}, u32[]{:S(2)}, u32[]{:S(2)}) collective-permute-start(f32[128,1024]{1,0:T(8,128)S(1)} %multiply_add_fusion.1), channel_id=1, source_target_pairs={{0,16},{16,0},{4,20},{20,4},{8,24},{24,8},{12,28},{28,12},{1,17},{... | collective-permute-start | bytes 1572872 | tf_op jit(solution)/shard_map/ppermute | solution.py:28
  272.1 22.1 %copy-start.10 = (f32[1024,256]{0,1:T(8,128)S(1)}, f32[1024,256]{0,1:T(8,128)}, u32[]{:S(2)}) copy-start(f32[1024,256]{0,1:T(8,128)} %copy-done.9) | copy-start | bytes 3145732
  272.1 22.1 %copy-start.15 = (f32[256,1024]{1,0:T(8,128)S(1)}, f32[256,1024]{1,0:T(8,128)}, u32[]{:S(2)}) copy-start(f32[256,1024]{1,0:T(8,128)} %copy-done.14) | copy-start | bytes 3145732
  294.2 1.4 copy-start.12
  294.2 2.8 copy-start.11
  295.8 7.0 %collective-permute-start.11 = (f32[3,256]{0,1:T(8,128)S(1)}, f32[3,256]{0,1:T(8,128)S(1)}, u32[]{:S(2)}, u32[]{:S(2)}) collective-permute-start(f32[3,256]{0,1:T(8,128)S(1)} %slice.380), channel_id=1, source_target_pairs={{4,0},{8,4},{12,8},{16,12},{20,16},{24,20},{28,24},{5,1},{9,5},{13... | collective-permute-start | bytes 9224 | tf_op jit(solution)/shard_map/ppermute | solution.py:18
  298.4 19.0 %collective-permute-start.10 = (f32[3,1024]{1,0:T(4,128)S(1)}, f32[3,1024]{1,0:T(4,128)S(1)}, u32[]{:S(2)}, u32[]{:S(2)}) collective-permute-start(f32[3,1024]{1,0:T(4,128)S(1)} %slice.375), channel_id=1, source_target_pairs={{4,0},{8,4},{12,8},{16,12},{20,16},{24,20},{28,24},{5,1},{9,5},{13... | collective-permute-start | bytes 36872 | tf_op jit(solution)/shard_map/ppermute | solution.py:18
where the time goes:
time: 322 us; the launch traced here: 319 us
  matrix products  121 us (38%)
  waiting for transfers between devices  71.4 us (22%)
  local copies, waits for them, and re-layouts  53.2 us (17%)
  other arithmetic  28.9 us (9%)
  starting transfers between devices  21.3 us (7%)
  blocking collectives  19.1 us (6%)
    dot_general x57, matrix products, matmul(): jnp.dot(left_mat, right_mat, precision=highest, preferred_element_type=jn...  121 us
    ppermute x8, waiting for transfers between devices, from_partner(): return lax.ppermute(block, axis, route)  68.3 us
    slice x32, local copies, waits for them, and re-layouts, head_mix(): weight_head[levels_id][:, None]  27.2 us
    psum x1, blocking collectives, per_device(): bc_grad = lax.psum(conv_backward(bc_slope, bc_next, conv_bc), 'head')  13.3 us
    ppermute x4, starting transfers between devices, shifted(): lax.ppermute(value, axis, [(source, source + steps) for source in range(i...  10.9 us
    ppermute x8, starting transfers between devices, from_partner(): return lax.ppermute(block, axis, route)  10.4 us
  transfers between devices with their start and end apart: 12, of which 6 were waited for; matrix products, arithmetic and copies ran while one was open for 50% of the time, Pallas kernels for 0%

commit v1 on v0

v1 whole, which is shorter than its diff:
```python
import functools

import jax
import jax.numpy as jnp
from jax import lax
from jax.experimental import pallas as pl
from jax.experimental.pallas import tpu as pltpu
from jax.sharding import PartitionSpec as P

HEADS = 64
HEAD_DIM = 64
STATE = 128
EPSILON = 1e-05
RIM = 16
F32 = jnp.float32
BF16 = jnp.bfloat16
HIGH = lax.Precision.HIGH
HIGHEST = lax.Precision.HIGHEST


def dot(a, b, contract=(1, 0), precision=HIGH):
    return lax.dot_general(
        a,
        b,
        (((contract[0],), (contract[1],)), ((), ())),
        precision=precision,
        preferred_element_type=F32,
    )


def split(value):
    high = value.astype(BF16)
    return high, (value - high.astype(F32)).astype(BF16)


def dot_exact(a, b, contract=(1, 0)):
    return lax.dot_general(
        a, b, (((contract[0],), (contract[1],)), ((), ())), preferred_element_type=F32
    )


def eye(size):
    row = lax.broadcasted_iota(jnp.int32, (size, size), 0)
    col = lax.broadcasted_iota(jnp.int32, (size, size), 1)
    return (row == col).astype(F32).astype(BF16)


def turn(value, identity):
    high, low = split(value)
    width = identity.shape[0]
    parts = []
    for at in range(0, value.shape[1], width):
        piece = slice(at, at + width)
        parts.append(
            dot_exact(identity, high[:, piece], (1, 1)) + dot_exact(identity, low[:, piece], (1, 1))
        )
    return parts[0] if len(parts) == 1 else jnp.concatenate(parts, axis=0)


def turn_exact(value, identity):
    width = identity.shape[0]
    parts = [
        dot_exact(identity, value[:, at : at + width], (1, 1))
        for at in range(0, value.shape[1], width)
    ]
    return parts[0] if len(parts) == 1 else jnp.concatenate(parts, axis=0)


def sigmoid(value):
    return 1.0 / (1.0 + jnp.exp(-value))


def by_head(rows, values):
    heads, width = rows.shape
    shaped = values.reshape(heads, values.shape[0] // heads, width)
    return (shaped * rows[:, None, :]).reshape(values.shape)


def call(body, outs, ins, scratch=(), flops=0):
    moved = sum(o.size * o.dtype.itemsize for o in (*outs, *ins))
    return pl.pallas_call(
        body,
        out_shape=[jax.ShapeDtypeStruct(o.shape, o.dtype) for o in outs],
        in_specs=[pl.BlockSpec(memory_space=pltpu.VMEM)] * len(ins),
        out_specs=[pl.BlockSpec(memory_space=pltpu.VMEM)] * len(outs),
        scratch_shapes=list(scratch),
        compiler_params=pltpu.CompilerParams(vmem_limit_bytes=40 * 2**20),
        cost_estimate=pl.CostEstimate(flops=flops, bytes_accessed=moved, transcendentals=0),
    )(*ins)


def shape(*dims, dtype=F32):
    return jax.ShapeDtypeStruct(dims, dtype)


def pre_kernel(
    x_ref, rim_ref, bc_ref, decay_ref, taps_x_ref, taps_bc_ref,
    xt_ref, slope_ref, bc_conv_ref, bct_ref, bc_slope_ref, cum_ref, sent_ref,
    xs_ref, bcs_ref,
):
    length, columns = x_ref.shape
    heads = decay_ref.shape[0]
    taps = taps_x_ref.shape[0]
    state = STATE
    first = RIM - taps + 1
    row = lax.broadcasted_iota(jnp.int32, (length, length), 0)
    col = lax.broadcasted_iota(jnp.int32, (length, length), 1)
    cum = dot(decay_ref[...], (row <= col).astype(F32), precision=HIGHEST)
    cum_ref[...] = cum
    total = cum[:, length - 1 :]
    end_weight = jnp.exp(total - cum)

    bcs_ref[:RIM] = rim_ref[:, columns:].astype(F32)
    bcs_ref[RIM:] = bc_ref[...].astype(F32)
    pre = sum(taps_bc_ref[k : k + 1] * bcs_ref[first + k : first + k + length] for k in range(taps))
    gate = sigmoid(pre)
    conv = pre * gate
    bc_conv_ref[...] = conv
    bc_slope_ref[...] = gate * (1.0 + pre * (1.0 - gate))
    identity = eye(128)
    bct_ref[...] = turn(conv, identity)
    b_high, b_low = split(conv[:, :state])
    b_both = jnp.concatenate([b_high, b_low], axis=1)

    xs_ref[:RIM] = rim_ref[:, :columns].astype(F32)
    xs_ref[RIM:] = x_ref[...].astype(F32)
    step = 128
    for at in range(0, columns, step):
        part = slice(at, at + step)
        pre = sum(
            taps_x_ref[k : k + 1, part] * xs_ref[first + k : first + k + length, part]
            for k in range(taps)
        )
        gate = sigmoid(pre)
        conv = pre * gate
        slope_ref[:, part] = gate * (1.0 + pre * (1.0 - gate))
        turned = turn(conv, identity)
        xt_ref[part] = turned
        at_head = at // HEAD_DIM
        weighted = by_head(end_weight[at_head : at_head + step // HEAD_DIM], turned)
        high, low = split(weighted)
        both = dot_exact(high, b_both)
        sent_ref[part] = both[:, :state] + both[:, state:] + dot_exact(low, b_high)
    sent_ref[columns:] = jnp.broadcast_to(total, (heads, state))


def over_heads(scales, values):
    return by_head(scales, values)


def upper_half(bit):
    return (lax.axis_index("ctx") // 2**bit) % 2 == 1


def join_kernel(bit, own_ref, other_ref, joined_ref):
    heads = own_ref.shape[0] // (HEAD_DIM + 1)
    columns = heads * HEAD_DIM
    upper = upper_half(bit)
    own_total, other_total = own_ref[columns:], other_ref[columns:]
    for_other = jnp.where(upper, jnp.exp(own_total), 1.0)
    for_own = jnp.where(upper, 1.0, jnp.exp(other_total))
    joined_ref[:columns] = over_heads(for_other, other_ref[:columns]) + over_heads(
        for_own, own_ref[:columns]
    )
    joined_ref[columns:] = own_total + other_total


def head_weights(head, cum_ref, cum_t, levels_ref, distance, causal):
    length = cum_ref.shape[1]
    half = length // 2
    low_bits = length.bit_length() - 1
    row = cum_ref[pl.ds(head, 1), :]
    lanes = lax.broadcasted_iota(jnp.int32, cum_t.shape, 1)
    col = jnp.sum(jnp.where(lanes == head, cum_t, 0.0), axis=1, keepdims=True)
    weights = [levels_ref[level, pl.ds(head, 1), :] for level in range(low_bits + 1)]
    blocks = []
    for at in (0, half):
        part = slice(at, at + half)
        chosen = jnp.broadcast_to(weights[0][:, part], (half, half))
        for level in range(1, low_bits):
            chosen = jnp.where(distance >= 2 ** (level - 1), weights[level][:, part], chosen)
        gap = jnp.where(causal, row[:, part] - col[part], -jnp.inf)
        blocks.append(chosen * jnp.exp(gap))
    late = slice(half, length)
    far = weights[low_bits][:, late] * jnp.exp(row[:, late] - col[:half])
    return blocks[0], far, blocks[1]


def block_masks(half):
    row = lax.broadcasted_iota(jnp.int32, (half, half), 0)
    col = lax.broadcasted_iota(jnp.int32, (half, half), 1)
    return jnp.bitwise_xor(row, col), col >= row


def scores_of(bct, state):
    return dot(bct[:state], bct[state:], (0, 0))


def intra_kernel(
    first_head, xt_ref, bct_ref, cum_ref, levels_ref, out_ref, scores_ref, cum_t_ref
):
    heads = out_ref.shape[0] // HEAD_DIM
    length = cum_ref.shape[1]
    half = length // 2
    scores_ref[...] = scores_of(bct_ref[...], STATE)
    cum_t_ref[...] = jnp.transpose(cum_ref[...])
    distance, causal = block_masks(half)

    def one(at, carry):
        head = first_head + at
        low, far, high = head_weights(
            head, cum_ref, cum_t_ref[...], levels_ref, distance, causal
        )
        values = xt_ref[pl.ds(pl.multiple_of(head * HEAD_DIM, HEAD_DIM), HEAD_DIM), :]
        to = pl.ds(pl.multiple_of(at * HEAD_DIM, HEAD_DIM), HEAD_DIM)
        early = low * scores_ref[:half, :half]
        late = jnp.concatenate([far, high], axis=0) * scores_ref[:, half:]
        out_ref[to, :half] = dot(values[:, :half], early)
        out_ref[to, half:] = dot(values, late)
        return carry

    lax.fori_loop(0, heads, one, 0)


def far_coefficients(bits, cum_ref, levels_ref, totals):
    length = cum_ref.shape[1]
    low_bits = length.bit_length() - 1
    last = levels_ref.shape[0] - 1
    decayed = jnp.exp(cum_ref[...])
    before = jnp.zeros(totals[0].shape, F32)
    rows = []
    for bit in range(bits):
        upper = upper_half(bit)
        scale = jnp.where(upper, jnp.exp(before), 0.0)[:, :1]
        rows.append(levels_ref[min(low_bits + 1 + bit, last)] * decayed * scale)
        before = before + jnp.where(upper, totals[bit], 0.0)
    return rows


def mixed_kernel(bits, pieces, *refs):
    came, refs = refs[:bits], refs[bits:]
    intra, refs = refs[:pieces], refs[pieces:]
    (bct_ref, cum_ref, levels_ref, gate_ref, grad_ref, gain_ref,
     mixed_ref, first_ref, second_ref, sums_ref, coef_ref) = refs
    columns, length = mixed_ref.shape
    state = STATE
    rows = far_coefficients(bits, cum_ref, levels_ref, [r[columns:] for r in came])
    for bit in range(bits):
        coef_ref[bit] = rows[bit]
    identity = eye(128)
    c_high, c_low = split(bct_ref[state:])
    square = jnp.zeros((8, length), F32)
    cross = jnp.zeros((8, length), F32)
    step = 128
    each = columns // pieces
    for at in range(0, columns, step):
        part = slice(at, at + step)
        at_head = slice(at // HEAD_DIM, (at + step) // HEAD_DIM)
        ssd = intra[at // each][at % each : at % each + step]
        for bit in range(bits):
            high, low = split(came[bit][part])
            seen = dot_exact(high, c_high) + dot_exact(low, c_high) + dot_exact(high, c_low)
            ssd = ssd + by_head(rows[bit][at_head], seen)
        gate = dot_exact(identity, gate_ref[:, part], (1, 1))
        gate = gate * sigmoid(gate)
        grad = dot_exact(identity, grad_ref[:, part], (1, 1)) * gain_ref[part]
        mixed = ssd * gate
        mixed_ref[part] = mixed
        first_ref[part] = gate * grad
        second_ref[part] = gate * mixed
        square = square + jnp.sum((mixed * mixed).reshape(step // 8, 8, length), axis=0)
        cross = cross + jnp.sum((grad * mixed).reshape(step // 8, 8, length), axis=0)
    sums_ref[0:1] = jnp.sum(square, axis=0, keepdims=True)
    sums_ref[1:2] = jnp.sum(cross, axis=0, keepdims=True)


def level_grad(grad, rows, c_both, c_high, state):
    high, low = split(by_head(rows, grad))
    both = dot_exact(high, c_both)
    return both[:, :state] + both[:, state:] + dot_exact(low, c_high)


def grad_kernel(inner, bits, sums_ref, first_ref, second_ref, bc_ref, coef_ref, grad_ref, level_ref):
    state = STATE
    columns = grad_ref.shape[0]
    inverse = lax.rsqrt(sums_ref[0:1] / inner + EPSILON)
    second = inverse * inverse * inverse * (sums_ref[1:2] / inner)
    c_high, c_low = split(bc_ref[:, state:])
    c_both = jnp.concatenate([c_high, c_low], axis=1)
    step = 128
    for at in range(0, columns, step):
        part = slice(at, at + step)
        at_head = slice(at // HEAD_DIM, (at + step) // HEAD_DIM)
        grad = first_ref[part] * inverse - second_ref[part] * second
        grad_ref[part] = grad
        level_ref[part] = level_grad(grad, coef_ref[bits - 1, at_head], c_both, c_high, state)


def out_kernel(inner, bits, sums_ref, mixed_ref, gain_ref, grad_ref, bc_ref, coef_ref, out_ref, *level_refs):
    state = STATE
    columns = grad_ref.shape[0]
    length = out_ref.shape[0]
    inverse = lax.rsqrt(sums_ref[0:1] / inner + EPSILON)
    c_high, c_low = split(bc_ref[:, state:])
    c_both = jnp.concatenate([c_high, c_low], axis=1)
    identity = eye(length)
    step = 128
    for at in range(0, columns, step):
        part = slice(at, at + step)
        at_head = slice(at // HEAD_DIM, (at + step) // HEAD_DIM)
        grad = grad_ref[part]
        for bit in range(bits - 1):
            level_refs[bit][part] = level_grad(grad, coef_ref[bit, at_head], c_both, c_high, state)
        normed = (gain_ref[part] * mixed_ref[part] * inverse).astype(BF16)
        out_ref[:, part] = dot_exact(identity, normed, (1, 1)).astype(BF16)


def intra_back_kernel(
    first_head, xt_ref, grad_ref, bct_ref, cum_ref, levels_ref, x_out_ref, scores_out_ref,
    scores_ref, cum_t_ref,
):
    heads = x_out_ref.shape[0] // HEAD_DIM
    length = cum_ref.shape[1]
    half = length // 2
    scores_ref[...] = scores_of(bct_ref[...], STATE)
    cum_t_ref[...] = jnp.transpose(cum_ref[...])
    distance, causal = block_masks(half)
    scores_out_ref[...] = jnp.zeros(scores_out_ref.shape, F32)

    def one(at, carry):
        head = first_head + at
        low, far, high = head_weights(
            head, cum_ref, cum_t_ref[...], levels_ref, distance, causal
        )
        where = pl.ds(pl.multiple_of(head * HEAD_DIM, HEAD_DIM), HEAD_DIM)
        values = xt_ref[where, :]
        grads = grad_ref[where, :]
        to = pl.ds(pl.multiple_of(at * HEAD_DIM, HEAD_DIM), HEAD_DIM)
        late = jnp.concatenate([far, high], axis=0)
        back = dot(grads[:, half:], late * scores_ref[:, half:], (1, 1))
        x_out_ref[to, :half] = back[:, :half] + dot(
            grads[:, :half], low * scores_ref[:half, :half], (1, 1)
        )
        x_out_ref[to, half:] = back[:, half:]
        outer = dot(values, grads, (0, 0))
        scores_out_ref[:half, :half] += outer[:half, :half] * low
        scores_out_ref[:, half:] += outer[:, half:] * late
        return carry

    lax.fori_loop(0, heads, one, 0)


def sent_back_kernel(bit, came_ref, level_ref, own_ref, other_ref, *refs):
    *next_refs, sent_ref, share_ref = refs
    heads = own_ref.shape[0] // (HEAD_DIM + 1)
    columns = heads * HEAD_DIM
    upper = upper_half(bit)
    total_grad = came_ref[...]
    if next_refs:
        total_grad = total_grad + next_refs[0][...]
    for_other = jnp.where(upper, jnp.exp(own_ref[columns:]), 1.0)
    for_own = jnp.where(upper, 1.0, jnp.exp(other_ref[columns:]))
    sent_ref[...] = over_heads(for_other, total_grad) + level_ref[...]
    share_ref[...] = over_heads(for_own, total_grad)


def bc_kernel(bits, *refs):
    came, refs = refs[:bits], refs[bits:]
    *score_refs, grad_ref, coef_ref, bct_ref, out_ref = refs
    state = STATE
    columns = grad_ref.shape[0]
    scores = sum(r[...] for r in score_refs)
    out_ref[:state] = dot(bct_ref[state:], scores, (1, 1))
    total = dot(bct_ref[:state], scores)
    identity = eye(state)
    step = 128
    for bit in range(bits):
        for at in range(0, columns, step):
            part = slice(at, at + step)
            at_head = slice(at // HEAD_DIM, (at + step) // HEAD_DIM)
            total = total + dot(
                turn(came[bit][part], identity), by_head(coef_ref[bit, at_head], grad_ref[part])
            )
    out_ref[state:] = total


def last_kernel(pieces, *refs):
    back, refs = refs[:pieces], refs[pieces:]
    (came_ref, share_ref, bct_ref, bct_grad_ref, xt_ref, cum_ref, slope_ref, bc_slope_ref,
     x_out_ref, bc_out_ref) = refs
    state = STATE
    columns, length = xt_ref.shape
    cum = cum_ref[...]
    end_weight = jnp.exp(cum[:, length - 1 :] - cum)
    b_high, b_low = split(bct_ref[:state])
    narrow = eye(state)
    wide = eye(length)
    step = 128
    each = columns // pieces
    b_grad = bct_grad_ref[:state]
    for at in range(0, columns, step):
        part = slice(at, at + step)
        rows = end_weight[at // HEAD_DIM : (at + step) // HEAD_DIM]
        came = came_ref[part] + share_ref[part]
        high, low = split(came)
        seen = dot_exact(high, b_high) + dot_exact(low, b_high) + dot_exact(high, b_low)
        total = back[at // each][at % each : at % each + step] + by_head(rows, seen)
        x_out_ref[:, part] = turn_rows(total, wide) * slope_ref[:, part]
        x_high, x_low = split(by_head(rows, xt_ref[part]))
        t_high = turn_rows_exact(high, narrow)
        t_low = turn_rows_exact(low, narrow)
        b_grad = b_grad + dot_exact(t_high, x_high) + dot_exact(t_high, x_low) + dot_exact(t_low, x_high)
    bc_grad = jnp.concatenate([b_grad, bct_grad_ref[state:]], axis=0)
    bc_out_ref[...] = turn_rows(bc_grad, wide) * bc_slope_ref[...]


def turn_rows(value, identity):
    high, low = split(value)
    return dot_exact(identity, high, (1, 1)) + dot_exact(identity, low, (1, 1))


def turn_rows_exact(value, identity):
    return dot_exact(identity, value, (1, 1)).astype(BF16)


def conv_back_kernel(slope_ref, next_ref, taps_ref, out_ref, rows_ref):
    length = slope_ref.shape[0]
    taps = taps_ref.shape[0]
    rows_ref[:length] = slope_ref[...]
    rows_ref[length:] = next_ref[...]
    out = sum(
        taps_ref[k : k + 1] * rows_ref[taps - 1 - k : taps - 1 - k + length] for k in range(taps)
    )
    out_ref[...] = out.astype(out_ref.dtype)


def shifted(value, axis, steps):
    count = lax.axis_size(axis)
    initial, last = (max(0, -steps), min(count, count - steps))
    return lax.ppermute(value, axis, [(source, source + steps) for source in range(initial, last)])


def partners(count, bit, up=True, down=True):
    route = []
    for low in range(count):
        high = low | 1 << bit
        if high != low and high < count:
            route += [(low, high)] * up + [(high, low)] * down
    return route


def per_device(
    x_raw, bc_raw, gate_raw, log_decay, level_weights, conv_x, conv_bc, norm_gain, out_grad
):
    length, columns = x_raw.shape
    heads = log_decay.shape[0]
    state = STATE
    count = lax.axis_size("ctx")
    bits = count.bit_length() - 1
    inner = HEADS * HEAD_DIM
    gain = norm_gain.reshape(columns, 1)

    tail = jnp.concatenate([x_raw[length - RIM :], bc_raw[length - RIM :]], axis=1)
    rim = shifted(tail, "ctx", 1)
    wide = shape(columns, length)
    xt, slope, bc_conv, bct, bc_slope, cum, own = call(
        pre_kernel,
        [wide, shape(length, columns), shape(length, 2 * state), shape(2 * state, length),
         shape(length, 2 * state), shape(heads, length), shape(columns + heads, state)],
        [x_raw, rim, bc_raw, log_decay, conv_x, conv_bc],
        scratch=[pltpu.VMEM((RIM + length, columns), F32), pltpu.VMEM((RIM + length, 2 * state), F32)],
    )

    pieces = max(bits, 1)
    while heads % pieces or (columns // pieces) % 128:
        pieces += 1
    each = columns // pieces
    intra_scratch = [pltpu.VMEM((length, length), F32), pltpu.VMEM((length, heads), F32)]
    intra = [
        call(
            functools.partial(intra_kernel, piece * heads // pieces),
            [shape(each, length)],
            [xt, bct, cum, level_weights],
            scratch=intra_scratch,
            flops=int(4e9) // pieces,
        )[0]
        for piece in range(pieces)
    ]

    owns, others = [own], []
    for bit in range(bits):
        top = bit == bits - 1
        other = lax.ppermute(owns[-1], "ctx", partners(count, bit, down=not top))
        others.append(other)
        if not top:
            owns += call(
                functools.partial(join_kernel, bit), [shape(columns + heads, state)], [owns[-1], other]
            )

    mixed, first, second, sums, coef = call(
        functools.partial(mixed_kernel, bits, pieces),
        [wide, wide, wide, shape(2, length), shape(bits, heads, length)],
        [*others, *intra, bct, cum, level_weights, gate_raw, out_grad, gain],
    )
    sums = lax.psum(sums, "head")
    grad, top_grad = call(
        functools.partial(grad_kernel, inner, bits),
        [wide, shape(columns, state)],
        [sums, first, second, bc_conv, coef],
    )
    came = lax.ppermute(top_grad, "ctx", partners(count, bits - 1, up=False))
    layer_out, *level_grads = call(
        functools.partial(out_kernel, inner, bits),
        [shape(length, columns, dtype=BF16)] + [shape(columns, state)] * (bits - 1),
        [sums, mixed, gain, grad, bc_conv, coef],
    )
    back = [
        call(
            functools.partial(intra_back_kernel, piece * heads // pieces),
            [shape(each, length), shape(length, length)],
            [xt, grad, bct, cum, level_weights],
            scratch=intra_scratch,
            flops=int(8e9) // pieces,
        )
        for piece in range(pieces)
    ]
    share = []
    for bit in range(bits - 2, -1, -1):
        sent, kept = call(
            functools.partial(sent_back_kernel, bit),
            [shape(columns, state), shape(columns, state)],
            [came, level_grads[bit], owns[bit], others[bit], *share],
        )
        share = [kept]
        came = lax.ppermute(sent, "ctx", partners(count, bit))
    (bct_grad,) = call(
        functools.partial(bc_kernel, bits),
        [shape(2 * state, length)],
        [*others, *[b[1] for b in back], grad, coef, bct],
        flops=int(2e9),
    )
    x_slope, bc_part = call(
        functools.partial(last_kernel, pieces),
        [shape(length, columns), shape(length, 2 * state)],
        [*[b[0] for b in back], came, share[0], bct, bct_grad, xt, cum, slope, bc_slope],
    )
    next_rows = shifted(jnp.concatenate([x_slope[:8], bc_part[:8]], axis=1), "ctx", -1)
    (x_grad,) = call(
        conv_back_kernel,
        [shape(length, columns, dtype=BF16)],
        [x_slope, next_rows[:, :columns], conv_x],
        scratch=[pltpu.VMEM((length + 8, columns), F32)],
    )
    (bc_grad,) = call(
        conv_back_kernel,
        [shape(length, 2 * state)],
        [bc_part, next_rows[:, columns:], conv_bc],
        scratch=[pltpu.VMEM((length + 8, 2 * state), F32)],
    )
    bc_grad = lax.psum(bc_grad, "head").astype(BF16)
    return layer_out, x_grad, bc_grad


def solution(mesh):
    in_specs = (
        P("ctx", "head"),
        P("ctx", None),
        P("ctx", "head"),
        P("head", "ctx"),
        P(None, "head", "ctx"),
        P(None, "head"),
        P(),
        P("head"),
        P("ctx", "head"),
    )
    out_specs = (P("ctx", "head"), P("ctx", "head"), P("ctx", None))
    return jax.shard_map(
        per_device, mesh=mesh, in_specs=in_specs, out_specs=out_specs, check_vma=False
    )
```

time: 322 us -> 145 us (0.45)
  matrix products: 121 us -> 0 us
  local copies, waits for them, and re-layouts: 53.2 us -> 11 us
  Pallas kernels: 0 us -> 33.4 us
  other arithmetic: 28.9 us -> 0.01 us
  waiting for transfers between devices: 71.4 us -> 44.4 us
  starting transfers between devices: 21.3 us -> 32.9 us
    dot_general x57 -> x0, matrix products: 121 us -> none  [matmul(): jnp.dot(left_mat, right_mat, precision=highest, preferred_element_type=jn...]
    pallas_call x0 -> x20, Pallas kernels: none -> 33.4 us  [call(): pl.pallas_call(body, out_shape=[jax.ShapeDtypeStruct(o.shape, o.dtype) fo...]
    slice x45 -> x8, local copies, waits for them, and re-layouts: 31.3 us -> 0.76 us  [the longest x2 0.74 us: per_device(): x_raw[length - RIM:]]
    ppermute x8 -> x6, waiting for transfers between devices: 68.3 us -> 38.2 us  [the longest x3 21 us: per_device(): other = lax.ppermute(owns[-1], 'ctx', partners(count, bit, down=not top))]
    ppermute x8 -> x6, starting transfers between devices: 10.4 us -> 26.7 us  [the longest x2 14.6 us: per_device(): came = lax.ppermute(sent, 'ctx', partners(count, bit))]
    mul x9 -> x0, other arithmetic: 14.2 us -> none  [the longest x3 6.44 us: fenwick_states(): upper_half * other_state * per_column(jnp.exp(before), head_dim)]
    add x4 -> x0, other arithmetic: 7.33 us -> none  [the longest x2 5.48 us: per_device(): upper_half * (other_stack + other_scale * stack_now)]
    while x2 -> x0, local copies, waits for them, and re-layouts: 5.23 us -> none  [the longest x1 2.68 us: per_device(): lax.fori_loop(0, head_count, intra_forward, jnp.zeros((length, columns),...]
  transfers between devices with their start and end apart: 12 -> 8, of which waited for: 6 -> 6; matrix products, arithmetic and copies ran while one was open for 50% -> 0% of each run, Pallas kernels for 0% -> 15%
where the time goes in v1:
time: 145 us
  waiting for transfers between devices  44.4 us (31%)
  Pallas kernels  33.4 us (23%)
  starting transfers between devices  32.9 us (23%)
  blocking collectives  21.8 us (15%)
  local copies, waits for them, and re-layouts  11 us (8%)
    pallas_call x20, Pallas kernels, call(): pl.pallas_call(body, out_shape=[jax.ShapeDtypeStruct(o.shape, o.dtype) fo...  33.4 us
    ppermute x3, waiting for transfers between devices, per_device(): other = lax.ppermute(owns[-1], 'ctx', partners(count, bit, down=not top))  21 us
    psum x1, blocking collectives, per_device(): bc_grad = lax.psum(bc_grad, 'head').astype(BF16)  16.1 us
    ppermute x2, starting transfers between devices, per_device(): came = lax.ppermute(sent, 'ctx', partners(count, bit))  14.6 us
    ppermute x1, waiting for transfers between devices, per_device(): came = lax.ppermute(top_grad, 'ctx', partners(count, bits - 1, up=False))  13.2 us
    ppermute x3, starting transfers between devices, per_device(): other = lax.ppermute(owns[-1], 'ctx', partners(count, bit, down=not top))  10.6 us
    unnamed x44, local copies, waits for them, and re-layouts  10.1 us
    ppermute x2, starting transfers between devices, shifted(): lax.ppermute(value, axis, [(source, source + steps) for source in range(i...  6.27 us
  transfers between devices with their start and end apart: 8, of which 6 were waited for; matrix products, arithmetic and copies ran while one was open for 0% of the time, Pallas kernels for 15%

profile of v1, /device:TPU:0, one launch (start us, length us, event | category | flops | bytes accessed | tf_op | source)
XLA Modules:
  0.0 144.6 jit_solution(10238441563262173081)
XLA Ops:
  0.6 0.0 slice-start
  0.6 0.0 slice-start.1
  0.7 0.7 slice-done
  1.4 0.0 slice-done.1
  1.4 5.0 %collective-permute-start = (bf16[16,1280]{1,0:T(8,128)(2,1)S(1)}, bf16[16,1280]{1,0:T(8,128)(2,1)S(1)}, u32[]{:S(2)}, u32[]{:S(2)}) collective-permute-start(bf16[16,1280]{1,0:T(8,128)(2,1)S(1)} %pad_maximum_fusion), channel_id=1, source_target_pairs={{0,4},{4,8},{8,12},{12,16},{16,20},{20,24},{24,28},{1,5},{5,9},{9,... | collective-permute-start | bytes 122888 | tf_op jit(solution)/shard_map/ppermute | solution.py:440
  6.4 1.7 %collective-permute-done.rim_ref = bf16[16,1280]{1,0:T(8,128)(2,1)S(1)} collective-permute-done((bf16[16,1280]{1,0:T(8,128)(2,1)S(1)}, bf16[16,1280]{1,0:T(8,128)(2,1)S(1)}, u32[]{:S(2)}, u32[]{:S(2)}) %collective-permute-start) | collective-permute-done | bytes 40992 | tf_op jit(solution)/shard_map/ppermute | solution.py:440
  8.1 0.0 copy-done.18
  8.1 0.0 copy-done.19
  8.1 0.0 copy-done.20
  8.1 1.0 copy-done.11
  9.1 0.9 copy-done.17
  10.0 2.3 %shard_map.112 = (f32[1024,256]{1,0:T(8,128)S(1)}, f32[256,1024]{1,0:T(8,128)S(1)}, f32[256,256]{1,0:T(8,128)S(1)}, f32[256,256]{1,0:T(8,128)S(1)}, f32[256,256]...) custom-call(bf16[256,1024]{1,0:T(8,128)(2,1)S(1)} %copy-done.11, ...), custom_call_target="tpu_custom_call" | custom-call | bytes 4165632 | tf_op jit(solution)/shard_map/pallas_call | solution.py:81
  12.4 0.0 copy-start.15
  12.4 0.7 copy-done.15
  13.1 2.3 %collective-permute-start.1 = (f32[1040,128]{1,0:T(8,128)S(1)}, f32[1040,128]{1,0:T(8,128)S(1)}, u32[]{:S(2)}, u32[]{:S(2)}) collective-permute-start(f32[1040,128]{1,0:T(8,128)S(1)} %get-tuple-element.34.own_ref), channel_id=1, source_target_pairs={{0,4},{4,0},{8,12},{12,8},{16,20},{20,16},{24,28},{28,24},{1,5},{5... | collective-permute-start | bytes 1597448 | tf_op jit(solution)/shard_map/ppermute | solution.py:493
  15.4 10.9 %collective-permute-done.1.other_ref.refs_0_ = f32[1040,128]{1,0:T(8,128)S(1)} collective-permute-done((f32[1040,128]{1,0:T(8,128)S(1)}, f32[1040,128]{1,0:T(8,128)S(1)}, u32[]{:S(2)}, u32[]{:S(2)}) %collective-permute-start.1) | collective-permute-done | bytes 532512 | tf_op jit(solution)/shard_map/ppermute | solution.py:493
  26.4 0.1 shard_map.113.own_ref
  26.5 0.0 copy-done
  26.5 2.8 %collective-permute-start.2 = (f32[1040,128]{1,0:T(8,128)S(1)}, f32[1040,128]{1,0:T(8,128)S(1)}, u32[]{:S(2)}, u32[]{:S(2)}) collective-permute-start(f32[1040,128]{1,0:T(8,128)S(1)} %shard_map.113.own_ref), channel_id=1, source_target_pairs={{0,8},{8,0},{4,12},{12,4},{16,24},{24,16},{20,28},{28,20},{1,9},{9... | collective-permute-start | bytes 1597448 | tf_op jit(solution)/shard_map/ppermute | solution.py:493
  29.3 10.0 %collective-permute-done.2.other_ref.refs_1_ = f32[1040,128]{1,0:T(8,128)S(1)} collective-permute-done((f32[1040,128]{1,0:T(8,128)S(1)}, f32[1040,128]{1,0:T(8,128)S(1)}, u32[]{:S(2)}, u32[]{:S(2)}) %collective-permute-start.2) | collective-permute-done | bytes 532512 | tf_op jit(solution)/shard_map/ppermute | solution.py:493
  39.3 0.9 shard_map.114
  40.2 5.4 %collective-permute-start.3 = (f32[1040,128]{1,0:T(8,128)}, f32[1040,128]{1,0:T(8,128)}, u32[]{:S(2)}, u32[]{:S(2)}) collective-permute-start(f32[1040,128]{1,0:T(8,128)} %shard_map.114), channel_id=1, source_target_pairs={{0,16},{4,20},{8,24},{12,28},{1,17},{5,21},{9,25},{13,29},{2,18},{... | collective-permute-start | bytes 1597448 | tf_op jit(solution)/shard_map/ppermute | solution.py:493
  45.7 0.2 copy.12.refs_12_.gain_ref
  45.9 0.7 copy-done.14
  46.6 1.2 copy-done.1
  47.8 1.6 %shard_map.118.refs_6_ = f32[256,256]{1,0:T(8,128)S(1)} custom-call(f32[1024,256]{1,0:T(8,128)S(1)} %copy-done.1, f32[256,256]{1,0:T(8,128)S(1)} %get-tuple-element.36.bct_ref.refs_7_.refs_9_.refs_6_, f32[16,256]{1,0:T(8,128)S(1)} %get-tuple-element.37.cum_ref.refs_8_.refs_9_, f32[16,16,256]{2,1,0:T(8,128)S(1)} %copy-done.14), custom_call_target="tpu_custom_call" | custom-call | flops 1000000000 | bytes 1851392 | tf_op jit(solution)/shard_map/pallas_call | solution.py:81
  49.4 1.6 %shard_map.117.refs_5_ = f32[256,256]{1,0:T(8,128)S(1)} custom-call(f32[1024,256]{1,0:T(8,128)S(1)} %copy-done.1, f32[256,256]{1,0:T(8,128)S(1)} %get-tuple-element.36.bct_ref.refs_7_.refs_9_.refs_6_, f32[16,256]{1,0:T(8,128)S(1)} %get-tuple-element.37.cum_ref.refs_8_.refs_9_, f32[16,16,256]{2,1,0:T(8,128)S(1)} %copy-done.14), custom_call_target="tpu_custom_call" | custom-call | flops 1000000000 | bytes 1851392 | tf_op jit(solution)/shard_map/pallas_call | solution.py:81
  50.9 1.5 %shard_map.116.refs_4_ = f32[256,256]{1,0:T(8,128)S(1)} custom-call(f32[1024,256]{1,0:T(8,128)S(1)} %copy-done.1, f32[256,256]{1,0:T(8,128)S(1)} %get-tuple-element.36.bct_ref.refs_7_.refs_9_.refs_6_, f32[16,256]{1,0:T(8,128)S(1)} %get-tuple-element.37.cum_ref.refs_8_.refs_9_, f32[16,16,256]{2,1,0:T(8,128)S(1)} %copy-done.14), custom_call_target="tpu_custom_call" | custom-call | flops 1000000000 | bytes 1851392 | tf_op jit(solution)/shard_map/pallas_call | solution.py:81
  52.5 0.0 copy-start.12
  52.5 0.0 copy-start.13
  52.5 1.5 %shard_map.115.refs_3_ = f32[256,256]{1,0:T(8,128)S(1)} custom-call(f32[1024,256]{1,0:T(8,128)S(1)} %copy-done.1, f32[256,256]{1,0:T(8,128)S(1)} %get-tuple-element.36.bct_ref.refs_7_.refs_9_.refs_6_, f32[16,256]{1,0:T(8,128)S(1)} %get-tuple-element.37.cum_ref.refs_8_.refs_9_, f32[16,16,256]{2,1,0:T(8,128)S(1)} %copy-done.14), custom_call_target="tpu_custom_call" | custom-call | flops 1000000000 | bytes 1851392 | tf_op jit(solution)/shard_map/pallas_call | solution.py:81
  54.1 0.0 collective-permute-done.3.refs_2_
  54.1 2.9 %shard_map.119 = (f32[1024,256]{1,0:T(8,128)S(1)}, f32[1024,256]{1,0:T(8,128)S(1)}, f32[1024,256]{1,0:T(8,128)S(1)}, f32[2,256]{1,0:T(2,128)S(1)}, f32[3,16,256]{2,1,0:T(8,128)S(1)}) custom-call(f32[1040,128]{1,0:T(8,128)S(1)} %collective-permute-done.1.other_ref.refs_0_, f32[1040,128]{1,0:T(8,128)S(1)} %collective-permute-done.2.other_ref.refs_1_, ...), custom_call_target="tpu_custom_call" | custom-call | bytes 7436288 | tf_op jit(solution)/shard_map/pallas_call | solution.py:81
  57.0 0.0 copy-start.5
  57.0 1.0 copy-done.5
  58.0 1.0 copy-done.7
  59.0 1.0 copy-done.9
  60.0 5.6 %psum.14.sums_ref = f32[2,256]{1,0:T(2,128)S(1)} all-reduce(f32[2,256]{1,0:T(2,128)S(1)} %get-tuple-element.38), channel_id=1, replica_groups=mesh['ctx'=8,'head'=4] {'head'}, use_global_device_ids=true, to_apply=%region_0.0 | all-reduce | flops 512 | bytes 4096 | tf_op jit(solution)/shard_map/psum | solution.py:505
  65.6 1.2 copy-done.8
  66.8 1.2 copy-done.10
  68.1 0.5 shard_map.120
  68.5 1.5 %collective-permute-start.4 = (f32[1024,128]{1,0:T(8,128)S(1)}, f32[1024,128]{1,0:T(8,128)S(1)}, u32[]{:S(2)}, u32[]{:S(2)}) collective-permute-start(f32[1024,128]{1,0:T(8,128)S(1)} %get-tuple-element.50), channel_id=1, source_target_pairs={{16,0},{20,4},{24,8},{28,12},{17,1},{21,5},{25,9},{29,13},{18,2},{... | collective-permute-start | bytes 1572872 | tf_op jit(solution)/shard_map/ppermute | solution.py:511
  70.0 1.8 %shard_map.121 = (bf16[256,1024]{1,0:T(8,128)(2,1)}, f32[1024,128]{1,0:T(8,128)S(1)}, f32[1024,128]{1,0:T(8,128)S(1)}) custom-call(f32[2,256]{1,0:T(2,128)S(1)} %psum.14.sums_ref, f32[1024,256]{1,0:T(8,128)S(1)} %copy-done.6, f32[1024,1]{1,0:T(8,128)S(1)} %copy.12.refs_12_.gain_ref, f32[1024,256]{1,0:T(8,128)S(1)} %get-tuple-element.44.grad_ref.refs_7_, ...), custom_call_target="tpu_custom_call" | custom-call | bytes 3987456 | tf_op jit(solution)/shard_map/pallas_call | solution.py:81
  71.8 13.2 %collective-permute-done.4.came_ref = f32[1024,128]{1,0:T(8,128)S(1)} collective-permute-done((f32[1024,128]{1,0:T(8,128)S(1)}, f32[1024,128]{1,0:T(8,128)S(1)}, u32[]{:S(2)}, u32[]{:S(2)}) %collective-permute-start.4) | collective-permute-done | bytes 524320 | tf_op jit(solution)/shard_map/ppermute | solution.py:511
  85.0 0.1 shard_map.126
  85.1 14.0 %collective-permute-start.5 = (f32[1024,128]{1,0:T(8,128)S(1)}, f32[1024,128]{1,0:T(8,128)S(1)}, u32[]{:S(2)}, u32[]{:S(2)}) collective-permute-start(f32[1024,128]{1,0:T(8,128)S(1)} %get-tuple-element.52), channel_id=1, source_target_pairs={{0,8},{8,0},{4,12},{12,4},{16,24},{24,16},{20,28},{28,20},{1,9},{9... | collective-permute-start | bytes 1572872 | tf_op jit(solution)/shard_map/ppermute | solution.py:535
  99.1 2.2 %shard_map.125 = (f32[256,256]{1,0:T(8,128)S(1)}, f32[256,256]{1,0:T(8,128)S(1)}) custom-call(f32[1024,256]{1,0:T(8,128)S(1)} %copy-done.2, f32[1024,256]{1,0:T(8,128)S(1)} %get-tuple-element.44.grad_ref.refs_7_, f32[256,256]{1,0:T(8,128)S(1)} %get-tuple-element.36.bct_ref.refs_7_.refs_9_.refs_6_, f32[16,256]{1,0:T(8,128)S(1)} %get-tuple-element.37.cum_ref.refs_8_.refs_9_, ...), custom_call_target="tpu_custom_call" | custom-call | flops 2000000000 | bytes 3162112 | tf_op jit(solution)/shard_map/pallas_call | solution.py:81
  101.3 2.2 %shard_map.124 = (f32[256,256]{1,0:T(8,128)S(1)}, f32[256,256]{1,0:T(8,128)S(1)}) custom-call(f32[1024,256]{1,0:T(8,128)S(1)} %copy-done.2, f32[1024,256]{1,0:T(8,128)S(1)} %get-tuple-element.44.grad_ref.refs_7_, f32[256,256]{1,0:T(8,128)S(1)} %get-tuple-element.36.bct_ref.refs_7_.refs_9_.refs_6_, f32[16,256]{1,0:T(8,128)S(1)} %get-tuple-element.37.cum_ref.refs_8_.refs_9_, ...), custom_call_target="tpu_custom_call" | custom-call | flops 2000000000 | bytes 3162112 | tf_op jit(solution)/shard_map/pallas_call | solution.py:81
  103.5 4.0 %collective-permute-done.5.came_ref = f32[1024,128]{1,0:T(8,128)S(1)} collective-permute-done((f32[1024,128]{1,0:T(8,128)S(1)}, f32[1024,128]{1,0:T(8,128)S(1)}, u32[]{:S(2)}, u32[]{:S(2)}) %collective-permute-start.5) | collective-permute-done | bytes 524320 | tf_op jit(solution)/shard_map/ppermute | solution.py:535
  107.5 0.2 shard_map.127
  107.7 0.6 collective-permute-start.6
  108.3 2.2 %shard_map.123 = (f32[256,256]{1,0:T(8,128)S(1)}, f32[256,256]{1,0:T(8,128)S(1)}) custom-call(f32[1024,256]{1,0:T(8,128)S(1)} %copy-done.2, f32[1024,256]{1,0:T(8,128)S(1)} %get-tuple-element.44.grad_ref.refs_7_, f32[256,256]{1,0:T(8,128)S(1)} %get-tuple-element.36.bct_ref.refs_7_.refs_9_.refs_6_, f32[16,256]{1,0:T(8,128)S(1)} %get-tuple-element.37.cum_ref.refs_8_.refs_9_, ...), custom_call_target="tpu_custom_call" | custom-call | flops 2000000000 | bytes 3162112 | tf_op jit(solution)/shard_map/pallas_call | solution.py:81
  110.5 2.2 %shard_map.122 = (f32[256,256]{1,0:T(8,128)S(1)}, f32[256,256]{1,0:T(8,128)S(1)}) custom-call(f32[1024,256]{1,0:T(8,128)S(1)} %copy-done.2, f32[1024,256]{1,0:T(8,128)S(1)} %get-tuple-element.44.grad_ref.refs_7_, f32[256,256]{1,0:T(8,128)S(1)} %get-tuple-element.36.bct_ref.refs_7_.refs_9_.refs_6_, f32[16,256]{1,0:T(8,128)S(1)} %get-tuple-element.37.cum_ref.refs_8_.refs_9_, ...), custom_call_target="tpu_custom_call" | custom-call | flops 2000000000 | bytes 3162112 | tf_op jit(solution)/shard_map/pallas_call | solution.py:81
  112.7 0.0 copy-start.16
  112.7 4.8 %shard_map.128.refs_7_ = f32[256,256]{1,0:T(8,128)S(1)} custom-call(f32[1040,128]{1,0:T(8,128)S(1)} %collective-permute-done.1.other_ref.refs_0_, f32[1040,128]{1,0:T(8,128)S(1)} %collective-permute-done.2.other_ref.refs_1_, f32[1040,128]{1,0:T(8,128)} %collective-permute-done.3.refs_2_, f32[256,256]{1,0:T(8,128)S(1)} %get-tuple-element.57.refs_3_, ...), custom_call_target="tpu_custom_call" | custom-call | flops 2000000000 | bytes 4268032 | tf_op jit(solution)/shard_map/pallas_call | solution.py:81
  117.5 0.0 collective-permute-done.6.refs_4_
  117.6 0.0 copy-done.4
  117.6 0.0 copy-done.16
  117.6 2.9 %shard_map.129 = (f32[256,1024]{1,0:T(8,128)S(1)}, f32[256,256]{1,0:T(8,128)S(1)}) custom-call(f32[256,256]{1,0:T(8,128)S(1)} %get-tuple-element.46.refs_0_, f32[256,256]{1,0:T(8,128)S(1)} %get-tuple-element.47.refs_1_, f32[256,256]{1,0:T(8,128)S(1)} %get-tuple-element.48.refs_2_, f32[256,256]{1,0:T(8,128)S(1)} %get-tuple-element.49.refs_3_, ...), custom_call_target="tpu_custom_call" | custom-call | bytes 6307840 | tf_op jit(solution)/shard_map/pallas_call | solution.py:81
  120.5 1.3 collective-permute-start.7
  121.8 4.6 %collective-permute-done.7 = f32[8,1280]{1,0:T(8,128)S(1)} collective-permute-done((f32[8,1280]{1,0:T(8,128)S(1)}, f32[8,1280]{1,0:T(8,128)S(1)}, u32[]{:S(2)}, u32[]{:S(2)}) %collective-permute-start.7) | collective-permute-done | bytes 40992 | tf_op jit(solution)/shard_map/ppermute | solution.py:440
  126.4 1.9 %shard_map.130 = bf16[256,1024]{1,0:T(8,128)(2,1)} custom-call(f32[256,1024]{1,0:T(8,128)S(1)} %get-tuple-element.63.slope_ref, f32[8,1024]{1,0:T(8,128)S(1)} %slice.24.next_ref, f32[4,1024]{1,0:T(4,128)S(1)} %copy-done.18), custom_call_target="tpu_custom_call" | custom-call | bytes 1622016 | tf_op jit(solution)/shard_map/pallas_call | solution.py:81
  128.2 0.2 shard_map.131
  128.5 16.1 %all-reduce.1 = bf16[256,256]{1,0:T(8,128)(2,1)} all-reduce(f32[256,256]{1,0:T(8,128)S(1)} %shard_map.131), channel_id=1, replica_groups=mesh['ctx'=8,'head'=4] {'head'}, use_global_device_ids=true, to_apply=%region_1.0 | all-reduce | flops 65536 | bytes 393216 | tf_op jit(solution)/shard_map/psum | solution.py:560
  (29 shorter events, 0.1 us)
Async XLA Ops:
  0.6 0.8 slice-start
  0.6 0.8 slice-start.1
  1.4 6.7 %copy-start.18 = (f32[4,1024]{1,0:T(4,128)S(1)}, f32[4,1024]{1,0:T(4,128)}, u32[]{:S(2)}) copy-start(f32[4,1024]{1,0:T(4,128)} %taps_ref.2) | copy-start | bytes 49156
  1.4 6.7 %copy-start.19 = (f32[4,256]{1,0:T(4,128)S(1)}, f32[4,256]{1,0:T(4,128)}, u32[]{:S(2)}) copy-start(f32[4,256]{1,0:T(4,128)} %taps_ref.3) | copy-start | bytes 12292
  1.4 6.7 %copy-start.20 = (f32[16,256]{1,0:T(8,128)S(1)}, f32[16,256]{1,0:T(8,128)}, u32[]{:S(2)}) copy-start(f32[16,256]{1,0:T(8,128)} %decay_ref.1) | copy-start | bytes 49156
  1.4 6.6 %collective-permute-start = (bf16[16,1280]{1,0:T(8,128)(2,1)S(1)}, bf16[16,1280]{1,0:T(8,128)(2,1)S(1)}, u32[]{:S(2)}, u32[]{:S(2)}) collective-permute-start(bf16[16,1280]{1,0:T(8,128)(2,1)S(1)} %pad_maximum_fusion), channel_id=1, source_target_pairs={{0,4},{4,8},{8,12},{12,16},{16,20},{20,24},{24,28},{1,5},{5,9},{9,... | collective-permute-start | bytes 122888 | tf_op jit(solution)/shard_map/ppermute | solution.py:440
  8.1 1.0 copy-start.11
  9.1 0.9 copy-start.17
  12.4 0.7 copy-start.15
  13.1 13.4 %copy-start = (f32[1024,256]{1,0:T(8,128)}, f32[1024,256]{1,0:T(8,128)S(1)}, u32[]{:S(2)}) copy-start(f32[1024,256]{1,0:T(8,128)S(1)} %get-tuple-element.35.xt_ref.refs_8_) | copy-start | bytes 3145732
  13.1 27.1 %copy-start.3 = (f32[256,1024]{1,0:T(8,128)}, f32[256,1024]{1,0:T(8,128)S(1)}, u32[]{:S(2)}) copy-start(f32[256,1024]{1,0:T(8,128)S(1)} %get-tuple-element.61.refs_10_) | copy-start | bytes 3145732
  13.1 13.3 %collective-permute-start.1 = (f32[1040,128]{1,0:T(8,128)S(1)}, f32[1040,128]{1,0:T(8,128)S(1)}, u32[]{:S(2)}, u32[]{:S(2)}) collective-permute-start(f32[1040,128]{1,0:T(8,128)S(1)} %get-tuple-element.34.own_ref), channel_id=1, source_target_pairs={{0,4},{4,0},{8,12},{12,8},{16,20},{20,16},{24,28},{28,24},{1,5},{5... | collective-permute-start | bytes 1597448 | tf_op jit(solution)/shard_map/ppermute | solution.py:493
  26.5 12.8 %collective-permute-start.2 = (f32[1040,128]{1,0:T(8,128)S(1)}, f32[1040,128]{1,0:T(8,128)S(1)}, u32[]{:S(2)}, u32[]{:S(2)}) collective-permute-start(f32[1040,128]{1,0:T(8,128)S(1)} %shard_map.113.own_ref), channel_id=1, source_target_pairs={{0,8},{8,0},{4,12},{12,4},{16,24},{24,16},{20,28},{28,20},{1,9},{9... | collective-permute-start | bytes 1597448 | tf_op jit(solution)/shard_map/ppermute | solution.py:493
  39.3 6.4 %copy-start.21 = (f32[1024]{0:T(1024)S(1)}, f32[1024]{0:T(1024)}, u32[]{:S(2)}) copy-start(f32[1024]{0:T(1024)} %param.16) | copy-start | bytes 12292
  40.2 13.9 %collective-permute-start.3 = (f32[1040,128]{1,0:T(8,128)}, f32[1040,128]{1,0:T(8,128)}, u32[]{:S(2)}, u32[]{:S(2)}) collective-permute-start(f32[1040,128]{1,0:T(8,128)} %shard_map.114), channel_id=1, source_target_pairs={{0,16},{4,20},{8,24},{12,28},{1,17},{5,21},{9,25},{13,29},{2,18},{... | collective-permute-start | bytes 1597448 | tf_op jit(solution)/shard_map/ppermute | solution.py:493
  45.6 1.0 copy-start.14
  46.6 1.2 copy-start.1
  52.5 1.6 %copy-start.12 = (bf16[256,1024]{1,0:T(8,128)(2,1)S(1)}, bf16[256,1024]{1,0:T(8,128)(2,1)}, u32[]{:S(2)}) copy-start(bf16[256,1024]{1,0:T(8,128)(2,1)} %refs_10_.1) | copy-start | bytes 1572868
  52.5 1.6 %copy-start.13 = (bf16[256,1024]{1,0:T(8,128)(2,1)S(1)}, bf16[256,1024]{1,0:T(8,128)(2,1)}, u32[]{:S(2)}) copy-start(bf16[256,1024]{1,0:T(8,128)(2,1)} %refs_11_.1) | copy-start | bytes 1572868
  57.0 1.0 copy-start.5
  58.0 1.0 copy-start.7
  59.0 1.0 copy-start.9
  65.6 1.2 copy-start.8
  66.8 1.2 copy-start.10
  68.1 2.0 %copy-start.6 = (f32[1024,256]{1,0:T(8,128)S(1)}, f32[1024,256]{1,0:T(8,128)}, u32[]{:S(2)}) copy-start(f32[1024,256]{1,0:T(8,128)} %copy-done.5) | copy-start | bytes 3145732
  68.5 16.5 %collective-permute-start.4 = (f32[1024,128]{1,0:T(8,128)S(1)}, f32[1024,128]{1,0:T(8,128)S(1)}, u32[]{:S(2)}, u32[]{:S(2)}) collective-permute-start(f32[1024,128]{1,0:T(8,128)S(1)} %get-tuple-element.50), channel_id=1, source_target_pairs={{16,0},{20,4},{24,8},{28,12},{17,1},{21,5},{25,9},{29,13},{18,2},{... | collective-permute-start | bytes 1572872 | tf_op jit(solution)/shard_map/ppermute | solution.py:511
  85.0 14.1 %copy-start.2 = (f32[1024,256]{1,0:T(8,128)S(1)}, f32[1024,256]{1,0:T(8,128)}, u32[]{:S(2)}) copy-start(f32[1024,256]{1,0:T(8,128)} %copy-done) | copy-start | bytes 3145732
  85.1 22.4 %collective-permute-start.5 = (f32[1024,128]{1,0:T(8,128)S(1)}, f32[1024,128]{1,0:T(8,128)S(1)}, u32[]{:S(2)}, u32[]{:S(2)}) collective-permute-start(f32[1024,128]{1,0:T(8,128)S(1)} %get-tuple-element.52), channel_id=1, source_target_pairs={{0,8},{8,0},{4,12},{12,4},{16,24},{24,16},{20,28},{28,20},{1,9},{9... | collective-permute-start | bytes 1572872 | tf_op jit(solution)/shard_map/ppermute | solution.py:535
  107.7 9.9 %collective-permute-start.6 = (f32[1024,128]{1,0:T(8,128)S(1)}, f32[1024,128]{1,0:T(8,128)S(1)}, u32[]{:S(2)}, u32[]{:S(2)}) collective-permute-start(f32[1024,128]{1,0:T(8,128)S(1)} %get-tuple-element.55), channel_id=1, source_target_pairs={{0,4},{4,0},{8,12},{12,8},{16,20},{20,16},{24,28},{28,24},{1,5},{5... | collective-permute-start | bytes 1572872 | tf_op jit(solution)/shard_map/ppermute | solution.py:535
  112.7 4.9 %copy-start.4 = (f32[256,1024]{1,0:T(8,128)S(1)}, f32[256,1024]{1,0:T(8,128)}, u32[]{:S(2)}) copy-start(f32[256,1024]{1,0:T(8,128)} %copy-done.3) | copy-start | bytes 3145732
  112.7 4.9 %copy-start.16 = (f32[256,256]{1,0:T(8,128)S(1)}, f32[256,256]{1,0:T(8,128)}, u32[]{:S(2)}) copy-start(f32[256,256]{1,0:T(8,128)} %copy-done.15) | copy-start | bytes 786436
  120.5 5.9 %collective-permute-start.7 = (f32[8,1280]{1,0:T(8,128)S(1)}, f32[8,1280]{1,0:T(8,128)S(1)}, u32[]{:S(2)}, u32[]{:S(2)}) collective-permute-start(f32[8,1280]{1,0:T(8,128)S(1)} %pad_maximum_fusion.1), channel_id=1, source_target_pairs={{4,0},{8,4},{12,8},{16,12},{20,16},{24,20},{28,24},{5,1},{9,5},{13... | collective-permute-start | bytes 122888 | tf_op jit(solution)/shard_map/ppermute | solution.py:440
